TPU v7x, 32 devices: a whole 2x2x4 slice. The times are simulated.
32 devices in a mesh: vloop: 4 (over z), pairs: 8 (over y, x, core).
Axes of the slice: x: 2, y: 2, z: 4, core: 2. Of those that a mesh axis runs over, the one named last changes fastest.
Arguments:
- factors: float32 [32, 512, 1280], P('vloop', 'pairs'), may hold values from -0.15625 to 0.15625
- amplitudes: float32 [512, 512, 128], P('vloop', 'pairs'), may hold values from -1 to 1
- occ_energy: float32 [96], replicated, may hold values from -2 to -0.5
- virt_energy: float32 [32], replicated, may hold values from 0.2 to 2.5
- pair_list: int32 [128, 2], P('pairs'), may hold values from 0 to 95
Outputs:
- new_amps: float32 [128, 32, 4, 8], P('pairs', 'vloop')
Inputs may be any that keep to these rules, and one draw needn't show every extreme that they name: `pair_list`: each entry names an occupied orbital.
All inputs are finite; a program needn't handle non-finite values.
Results may differ from a plain program's by a relative error of at most 0.00016.
Values sent between devices are 32-bit elements; how exact they have to be, the bound alone decides.
A program may use at most 192 MiB of HBM per device.

v0:
```python
import jax
import jax.numpy as jnp
from jax import lax
from jax.sharding import PartitionSpec as P

STEPS = 4


def shifted(shard, axis, by):
    count = lax.axis_size(axis)
    return lax.ppermute(shard, axis, [(i, (i + by) % count) for i in range(count)])


def local(factors, amplitudes, occ_energy, virt_energy, pair_list):
    loop_size = lax.axis_size("vloop")
    loop_index = lax.axis_index("vloop")
    rows_dev, slice_cols, aux_count = factors.shape
    all_amps = lax.all_gather(amplitudes, "vloop", axis=0, tiled=True)
    slab_list = []
    current = factors
    slab_list.append(current)
    for step_index in range(1, STEPS):
        current = shifted(current, "vloop", 1)
        slab_list.append(current)
    stacked = jnp.stack(slab_list, axis=0)
    slab_matrix = stacked.reshape(STEPS * rows_dev * slice_cols, aux_count)
    shard_piece = lax.all_gather(factors, "pairs", axis=1, tiled=True)
    piece_cols = shard_piece.shape[1]
    integrals = lax.dot_general(
        shard_piece.reshape(rows_dev * piece_cols, aux_count),
        slab_matrix,
        (((1,), (1,)), ((), ())),
        precision=lax.Precision.HIGHEST,
        preferred_element_type=jnp.float32,
    )
    integrals = integrals.reshape(rows_dev, piece_cols, STEPS, rows_dev, slice_cols)
    ladder = jnp.einsum("acsbd,cdp->pasb", integrals, all_amps, precision=lax.Precision.HIGHEST)
    summed = lax.psum_scatter(ladder, "pairs", scatter_dimension=0, tiled=True)
    one_hot = (
        pair_list[:, :, None] == jnp.arange(occ_energy.shape[0], dtype=jnp.int32)[None, None, :]
    ).astype(jnp.float32)
    occ_pair = jnp.sum(one_hot * occ_energy[None, None, :], axis=(1, 2))
    energy_a = lax.dynamic_slice_in_dim(virt_energy, loop_index * rows_dev, rows_dev)
    partner_list = []
    for step_index in range(STEPS):
        owner_block = jnp.mod(loop_index - step_index + loop_size, loop_size)
        partner_list.append(lax.dynamic_slice_in_dim(virt_energy, owner_block * rows_dev, rows_dev))
    energy_b = jnp.stack(partner_list, axis=0)
    denominator = (
        energy_a[None, :, None, None] + energy_b[None, None, :, :] - occ_pair[:, None, None, None]
    )
    return summed / denominator


def solution(mesh):
    placed = (P("vloop", "pairs", None), P("vloop", "pairs", None), P(), P(), P("pairs", None))
    return jax.shard_map(
        local,
        mesh=mesh,
        in_specs=placed,
        out_specs=P("pairs", "vloop", None, None),
        check_vma=False,
    )
```

profile of v0, /device:TPU:0, one launch (start us, length us, event | category | flops | bytes accessed | tf_op | source)
XLA Modules:
  0.0 571.0 jit_solution(17432736266080478027)
XLA Ops:
  6.5 0.0 copy-start
  6.5 0.0 copy-start.2
  6.5 0.0 copy-start.4
  6.5 0.0 copy-start.3
  6.5 0.0 all-gather.3.cloned.1.call-start
  6.6 0.7 all-gather.3.cloned.1.call-update
  7.3 0.0 all-gather.5.cloned.1.call-start
  7.3 6.7 %copy.12 = f32[128,64,128]{2,0,1:T(8,128)} copy(f32[128,64,128]{2,1,0:T(8,128)} %param.6) | data formatting | bytes 8388608 | tf_op args[1]
  14.0 0.0 all-gather.5.cloned.1.call-update
  14.0 0.0 reduce-scatter.4.cloned.1.call-start
  14.1 0.0 copy-done
  14.1 3.1 collective-permute-start
  17.1 58.9 %collective-permute-done = f32[8,64,1280]{2,1,0:T(8,128)S(1)} collective-permute-done((f32[8,64,1280]{2,1,0:T(8,128)S(1)}, f32[8,64,1280]{2,1,0:T(8,128)S(1)}, u32[]{:S(2)}, u32[]{:S(2)}) %collective-permute-start) | collective-permute-done | bytes 2621472 | tf_op jit(solution)/shard_map/ppermute | solution.py:11
  76.0 0.0 copy-start.1
  76.0 1.5 copy-done.1
  77.5 0.0 collective-permute-start.1
  77.5 60.1 %collective-permute-done.1 = f32[8,64,1280]{2,1,0:T(8,128)} collective-permute-done((f32[8,64,1280]{2,1,0:T(8,128)S(1)}, f32[8,64,1280]{2,1,0:T(8,128)}, u32[]{:S(2)}, u32[]{:S(2)}) %collective-permute-start.1) | collective-permute-done | bytes 2621472 | tf_op jit(solution)/shard_map/ppermute | solution.py:11
  137.6 0.0 collective-permute-start.2
  137.6 0.0 copy-done.2
  137.6 0.1 fusion.5
  137.7 0.0 copy-done.4
  137.7 0.0 copy-done.3
  137.7 0.2 select_reduce_fusion
  137.9 116.9 %collective-permute-done.2 = f32[8,64,1280]{2,1,0:T(8,128)} collective-permute-done((f32[8,64,1280]{2,1,0:T(8,128)}, f32[8,64,1280]{2,1,0:T(8,128)}, u32[]{:S(2)}, u32[]{:S(2)}) %collective-permute-start.2) | collective-permute-done | bytes 2621472 | tf_op jit(solution)/shard_map/ppermute | solution.py:11
  254.7 6.5 %pad_maximum_fusion = f32[4,8,64,1280]{3,2,1,0:T(8,128)} fusion(f32[1,8,64,1280]{3,2,1,0:T(8,128)} %bitcast.3, f32[1,8,64,1280]{3,2,1,0:T(8,128)} %bitcast.2, f32[1,8,64,1280]{3,2,1,0:T(8,128)} %bitcast.41, f32[1,8,64,1280]{3,2,1,0:T(8,128)S(1)} %bitcast.39), kind=kLoop, calls=%fused_computation.2 | loop fusion | flops 7864320 | bytes 20971520 | tf_op jit(solution)/shard_map/stack | solution.py:25
  261.2 0.0 all-gather.3.cloned.1.call-done
  261.2 141.4 %fusion.6 = f32[2048,4096]{1,0:T(8,128)} fusion(f32[2048,1280]{1,0:T(8,128)} %bitcast.40, f32[4096,1280]{1,0:T(8,128)} %bitcast.43), kind=kOutput, calls=%fused_computation.14 | convolution fusion | flops 128849018880 | bytes 65011712 | tf_op jit(solution)/shard_map/dot_general | solution.py:29
  402.6 37.9 %copy.20 = f32[256,8,8,512]{3,2,1,0:T(8,128)} copy(f32[256,8,8,512]{3,1,2,0:T(8,128)} %bitcast.38) | data formatting | bytes 67108864
  440.5 23.5 %all-gather.5.cloned.1.call-done = f32[512,64,128]{2,0,1:T(8,128)} async-done(((f32[128,64,128]{2,0,1:T(8,128)}), f32[512,64,128]{2,0,1:T(8,128)}) %all-gather.5.cloned.1.call-update) | async-done | bytes 16777232 | tf_op jit(solution)/shard_map/all_gather | solution.py:18
  464.0 31.7 %fusion.2 = f32[128,8,4,8]{0,1,3,2:T(8,128)S(1)} fusion(f32[8,512,4,8,64]{1,0,4,3,2:T(8,128)} %bitcast.37, f32[512,64,128]{2,0,1:T(8,128)} %all-gather.5.cloned.1.call-done), kind=kOutput, calls=%fused_computation.3 | convolution fusion | flops 12884901888 | bytes 50462720 | tf_op jit(solution)/shard_map/acsbd,cdp->pasb/dot_general | solution.py:37
  495.8 2.2 copy.16
  498.0 3.1 reshape.25
  501.1 0.0 reduce-scatter.4.cloned.1.call-update
  501.2 0.1 broadcast_add_fusion
  501.2 61.6 %reduce-scatter.4.cloned.1.call-done = f32[16,256]{1,0:T(8,128)} async-done(((f32[128,256]{1,0:T(8,128)}), f32[16,256]{1,0:T(8,128)}) %reduce-scatter.4.cloned.1.call-update) | async-done | bytes 16400
  562.9 0.8 copy.19
  563.7 0.8 subtract_divide_fusion
  (1 shorter events, 0.0 us)
Async XLA Ops:
  6.5 7.5 %copy-start = (f32[8,64,1280]{2,1,0:T(8,128)S(1)}, f32[8,64,1280]{2,1,0:T(8,128)}, u32[]{:S(2)}) copy-start(f32[8,64,1280]{2,1,0:T(8,128)} %param.5) | copy-start | bytes 7864324
  6.5 131.0 %copy-start.2 = (f32[32]{0:T(128)S(1)}, f32[32]{0:T(128)}, u32[]{:S(2)}) copy-start(f32[32]{0:T(128)} %param.8) | copy-start | bytes 388
  6.5 131.1 %copy-start.4 = (f32[96]{0:T(128)S(1)}, f32[96]{0:T(128)}, u32[]{:S(2)}) copy-start(f32[96]{0:T(128)} %param.7) | copy-start | bytes 1156
  6.5 131.1 %copy-start.3 = (s32[16,2]{0,1:T(2,128)S(1)}, s32[16,2]{0,1:T(2,128)}, u32[]{:S(2)}) copy-start(s32[16,2]{0,1:T(2,128)} %param.9) | copy-start | bytes 388
  6.5 254.7 %all-gather.3.cloned.1.call-start = ((), (), s32[]{:S(2)}) async-start(), calls=%async_computation.1 | async-start | bytes 23592960 | tf_op jit(solution)/shard_map/all_gather | solution.py:27
  7.3 456.8 %all-gather.5.cloned.1.call-start = ((), (), s32[]{:S(2)}) async-start(), calls=%async_computation.2 | async-start | bytes 20971520 | tf_op jit(solution)/shard_map/all_gather | solution.py:18
  14.0 548.9 %reduce-scatter.4.cloned.1.call-start = ((), (), s32[]{:S(2)}) async-start(), calls=%async_computation.3 | async-start | bytes 147456
  14.1 62.0 %collective-permute-start = (f32[8,64,1280]{2,1,0:T(8,128)S(1)}, f32[8,64,1280]{2,1,0:T(8,128)S(1)}, u32[]{:S(2)}, u32[]{:S(2)}) collective-permute-start(f32[8,64,1280]{2,1,0:T(8,128)S(1)} %copy-done), channel_id=1, source_target_pairs={{0,8},{8,16},{16,24},{24,0},{1,9},{9,17},{17,25},{25,1},{2,10},{10... | collective-permute-start | bytes 7864328 | tf_op jit(solution)/shard_map/ppermute | solution.py:11
  76.0 1.5 copy-start.1
  77.5 60.1 %collective-permute-start.1 = (f32[8,64,1280]{2,1,0:T(8,128)S(1)}, f32[8,64,1280]{2,1,0:T(8,128)}, u32[]{:S(2)}, u32[]{:S(2)}) collective-permute-start(f32[8,64,1280]{2,1,0:T(8,128)S(1)} %collective-permute-done), channel_id=1, source_target_pairs={{0,8},{8,16},{16,24},{24,0},{1,9},{9,17},{17,25},{25,1},{2,10},{10... | collective-permute-start | bytes 7864328 | tf_op jit(solution)/shard_map/ppermute | solution.py:11
  137.6 117.2 %collective-permute-start.2 = (f32[8,64,1280]{2,1,0:T(8,128)}, f32[8,64,1280]{2,1,0:T(8,128)}, u32[]{:S(2)}, u32[]{:S(2)}) collective-permute-start(f32[8,64,1280]{2,1,0:T(8,128)} %collective-permute-done.1), channel_id=1, source_target_pairs={{0,8},{8,16},{16,24},{24,0},{1,9},{9,17},{17,25},{25,1},{2,10},{10... | collective-permute-start | bytes 7864328 | tf_op jit(solution)/shard_map/ppermute | solution.py:11
Sparse Core Ops, SparseCore 0:
  9.3 110.2 all-gather.2
  121.2 342.8 all-gather.4
  501.3 61.5 reduce-scatter.3
where the time goes:
time: 571 us
  waiting for transfers between devices  322 us (56%)
  matrix products  173 us (30%)
  local copies, waits for them, and re-layouts  52.3 us (9%)
  between operations  13.2 us (2%)
  other arithmetic  7.52 us (1%)
    ppermute x3, waiting for transfers between devices, shifted(): lax.ppermute(shard, axis, [(i, (i + by) % count) for i in range(count)])  236 us
    dot_general x1, matrix products, local(): lax.dot_general(shard_piece.reshape(rows_dev * piece_cols, aux_count), sl...  141 us
    unnamed x4, waiting for transfers between devices  62.3 us
    unnamed x15, local copies, waits for them, and re-layouts  52.2 us
    dot_general x1, matrix products, local(): jnp.einsum('acsbd,cdp->pasb', integrals, all_amps, precision=lax.Precisio...  31.7 us
    all_gather x1, waiting for transfers between devices, local(): all_amps = lax.all_gather(amplitudes, 'vloop', axis=0, tiled=True)  23.5 us
  transfers between devices with their start and end apart: 6, of which 5 were waited for; matrix products, arithmetic and copies ran while one was open for 34% of the time, Pallas kernels for 0%

commit v1 on v0

v1 whole, which is shorter than its diff:
```python
import functools

import jax
import jax.numpy as jnp
from jax import lax
from jax.experimental import pallas as pl
from jax.experimental.pallas import tpu as pltpu
from jax.sharding import PartitionSpec as P

STEPS = 4
LANES = 128
WIDE = 256
NT = (((1,), (1,)), ((), ()))
NN = (((1,), (0,)), ((), ()))


def split(value):
    high = value.astype(jnp.bfloat16)
    return high, (value - high.astype(jnp.float32)).astype(jnp.bfloat16)


def product(left, right, dims):
    dot = functools.partial(
        lax.dot_general, dimension_numbers=dims, preferred_element_type=jnp.float32
    )
    return dot(left[0], right[0]) + (dot(left[0], right[1]) + dot(left[1], right[0]))


def ladder_kernel(count, row_ref, amp_ref, *refs):
    cols, (out_ref, high_ref, low_ref, held_ref) = refs[:count], refs[count:]
    rows, tile, aux = row_ref.shape
    width = cols[0].shape[0]
    depth = amp_ref.shape[1]
    group = LANES // depth
    fold = WIDE // LANES

    @pl.when(pl.program_id(0) == 0)
    def _():
        out_ref[...] = jnp.zeros_like(out_ref)
        for i in range(count):
            high, low = split(cols[i][...])
            high_ref[pl.ds(i * width, width), :] = high
            low_ref[pl.ds(i * width, width), :] = low

    left = split(row_ref[...].reshape(rows * tile, aux))
    for i in range(count):
        at = pl.ds(i * width, width)
        part = product(left, (high_ref[at, :], low_ref[at, :]), NT)
        for b in range(width // LANES):
            held_ref[i * (width // LANES) + b] = part[:, b * LANES : (b + 1) * LANES]

    total = out_ref[...]
    for c in range(0, tile, fold):
        weights = []
        for k in range(fold):
            amp = amp_ref[c + k]
            blank = jnp.zeros_like(amp)
            for g in range(group):
                weights.append(
                    jnp.concatenate([amp if h == g else blank for h in range(group)], axis=1)
                )
        right = split(jnp.concatenate(weights, axis=0))
        pieces = []
        for b in range(count * width // LANES):
            pieces.append(
                jnp.concatenate(
                    [
                        held_ref[b, pl.ds(c + k, rows, stride=tile), :]
                        for k in range(fold)
                    ],
                    axis=1,
                )
            )
        total = total + product(split(jnp.concatenate(pieces, axis=0)), right, NN)
    out_ref[...] = total


def ladder_part(row_side, amplitudes, cols):
    rows, all_c, aux = row_side.shape
    _, depth, pair_count = amplitudes.shape
    count = len(cols)
    width = cols[0].shape[0] * cols[0].shape[1]
    group = LANES // depth
    tile = max(8, 512 // rows)
    height = count * width // LANES * rows
    out = pl.pallas_call(
        functools.partial(ladder_kernel, count),
        grid=(all_c // tile,),
        out_shape=jax.ShapeDtypeStruct((height, group * pair_count), jnp.float32),
        in_specs=[
            pl.BlockSpec((rows, tile, aux), lambda i: (0, i, 0)),
            pl.BlockSpec((tile, depth, pair_count), lambda i: (i, 0, 0)),
        ]
        + [
            pl.BlockSpec((width, aux), lambda i: (0, 0), pipeline_mode=pl.Buffered(1))
        ] * count,
        out_specs=pl.BlockSpec((height, group * pair_count), lambda i: (0, 0)),
        scratch_shapes=[
            pltpu.VMEM((count * width, aux), jnp.bfloat16),
            pltpu.VMEM((count * width, aux), jnp.bfloat16),
            pltpu.VMEM((count * width // LANES, rows * tile, LANES), jnp.float32),
        ],
        compiler_params=pltpu.CompilerParams(vmem_limit_bytes=56 * 2**20),
        cost_estimate=pl.CostEstimate(
            flops=6 * rows * all_c * count * width * (aux + group * pair_count),
            bytes_accessed=4 * (rows * all_c * aux + count * width * aux),
            transcendentals=0,
        ),
    )(row_side, amplitudes, *[col.reshape(width, aux) for col in cols])
    out = out.reshape(count * width // LANES, rows, group, pair_count)
    return out.transpose(0, 2, 1, 3).reshape(count, -1, rows, pair_count)


def local(factors, amplitudes, occ_energy, virt_energy, pair_list):
    loop_size = lax.axis_size("vloop")
    pair_size = lax.axis_size("pairs")
    loop_index = lax.axis_index("vloop")
    rows_dev, slice_cols, aux_count = factors.shape
    pair_count = amplitudes.shape[2]
    block_cols = amplitudes.shape[0]
    per_block = pair_size // loop_size
    rows_each = max(1, rows_dev // pair_size)
    cols_each = rows_dev * slice_cols // (pair_size * rows_each)
    chunk = rows_each * cols_each

    spread = lax.all_to_all(factors.reshape(pair_size, chunk, aux_count), "pairs", 0, 0)
    spread = lax.all_to_all(
        spread.reshape(loop_size, per_block, chunk, aux_count), "vloop", 0, 0
    )
    row_side = lax.all_gather(
        spread.reshape(loop_size, 1, per_block * chunk, aux_count), "pairs", axis=1, tiled=True
    )
    row_side = row_side.reshape(
        loop_size,
        rows_dev // rows_each,
        slice_cols // cols_each,
        per_block,
        rows_each,
        cols_each,
        aux_count,
    )
    row_side = row_side.transpose(0, 1, 4, 3, 2, 5, 6)
    row_side = row_side.reshape(loop_size * rows_dev, block_cols, aux_count)

    def shifted(by):
        if by == 0:
            return factors
        return lax.ppermute(factors, "vloop", [(i, (i + by) % loop_size) for i in range(loop_size)])

    order = [0, 1, loop_size - 1] + list(range(2, loop_size - 1))
    half = loop_size // 2
    found = {}
    for start in (0, half):
        shifts = order[start : start + half]
        part = ladder_part(row_side, amplitudes, [shifted(by) for by in shifts])
        for i, by in enumerate(shifts):
            found[by] = part[i]
    stacked = jnp.stack([found[by] for by in range(loop_size)])
    blocks = [
        lax.dynamic_index_in_dim(stacked, jnp.mod(loop_index - w + loop_size, loop_size), 0, False)
        for w in range(loop_size)
    ]
    rows = []
    for z in range(loop_size):
        mine = jnp.stack([blocks[(z - s) % loop_size] for s in range(STEPS)])
        mine = mine[:, :, z * rows_dev : (z + 1) * rows_dev]
        rows.append(mine.transpose(3, 2, 0, 1))
    ladder = jnp.concatenate(rows, axis=1)
    summed = lax.psum_scatter(ladder, "pairs", scatter_dimension=0, tiled=True)
    summed = lax.psum_scatter(summed, "vloop", scatter_dimension=1, tiled=True)

    one_hot = (
        pair_list[:, :, None] == jnp.arange(occ_energy.shape[0], dtype=jnp.int32)[None, None, :]
    ).astype(jnp.float32)
    occ_pair = jnp.sum(one_hot * occ_energy[None, None, :], axis=(1, 2))
    energy_a = lax.dynamic_slice_in_dim(virt_energy, loop_index * rows_dev, rows_dev)
    partner_list = []
    for step_index in range(STEPS):
        owner_block = jnp.mod(loop_index - step_index + loop_size, loop_size)
        partner_list.append(lax.dynamic_slice_in_dim(virt_energy, owner_block * rows_dev, rows_dev))
    energy_b = jnp.stack(partner_list, axis=0)
    denominator = (
        energy_a[None, :, None, None] + energy_b[None, None, :, :] - occ_pair[:, None, None, None]
    )
    return summed / denominator


def solution(mesh):
    placed = (P("vloop", "pairs", None), P("vloop", "pairs", None), P(), P(), P("pairs", None))
    return jax.shard_map(
        local,
        mesh=mesh,
        in_specs=placed,
        out_specs=P("pairs", "vloop", None, None),
        check_vma=False,
    )
```

time: 571 us -> 543 us (0.951)
  matrix products: 173 us -> 0 us
  Pallas kernels: 0 us -> 119 us
  blocking collectives: 0 us -> 101 us
  waiting for transfers between devices: 322 us -> 283 us
  local copies, waits for them, and re-layouts: 52.3 us -> 17 us
    dot_general x2 -> x0, matrix products: 173 us -> none  [the longest x1 141 us: local(): lax.dot_general(shard_piece.reshape(rows_dev * piece_cols, aux_count), sl...]
    pallas_call x0 -> x2, Pallas kernels: none -> 119 us  [ladder_part(): pl.pallas_call(functools.partial(ladder_kernel, count), grid=(all_c // ti...]
    all_to_all x0 -> x2, blocking collectives: none -> 101 us  [the longest x1 63.6 us: local(): lax.all_to_all(spread.reshape(loop_size, per_block, chunk, aux_count), 'v...]
    unnamed x4 -> x3, waiting for transfers between devices: 62.3 us -> 0.05 us
    reduce_scatter x0 -> x2, waiting for transfers between devices: none -> 59.7 us  [the longest x1 38.1 us: local(): summed = lax.psum_scatter(ladder, 'pairs', scatter_dimension=0, tiled=True)]
    unnamed x15 -> x8, local copies, waits for them, and re-layouts: 52.2 us -> 2.21 us
    all_gather x2 -> x1, waiting for transfers between devices: 23.5 us -> 0.01 us  [local(): lax.all_gather(spread.reshape(loop_size, 1, per_block * chunk, aux_count)...]
    ppermute x3, waiting for transfers between devices: 236 us -> 223 us  [shifted(): lax.ppermute(factors, 'vloop', [(i, (i + by) % loop_size) for i in range(...]
  transfers between devices with their start and end apart: 6 -> 6, of which waited for: 5 -> 4; matrix products, arithmetic and copies ran while one was open for 34% -> 0% of each run, Pallas kernels for 0% -> 11%
where the time goes in v1:
time: 543 us
  waiting for transfers between devices  283 us (52%)
  Pallas kernels  119 us (22%)
  blocking collectives  101 us (19%)
  local copies, waits for them, and re-layouts  17 us (3%)
  between operations  13.3 us (2%)
  other arithmetic  7.9 us (1%)
    ppermute x3, waiting for transfers between devices, shifted(): lax.ppermute(factors, 'vloop', [(i, (i + by) % loop_size) for i in range(...  223 us
    pallas_call x2, Pallas kernels, ladder_part(): pl.pallas_call(functools.partial(ladder_kernel, count), grid=(all_c // ti...  119 us
    all_to_all x1, blocking collectives, local(): lax.all_to_all(spread.reshape(loop_size, per_block, chunk, aux_count), 'v...  63.6 us
    reduce_scatter x1, waiting for transfers between devices, local(): summed = lax.psum_scatter(ladder, 'pairs', scatter_dimension=0, tiled=True)  38.1 us
    all_to_all x1, blocking collectives, local(): lax.all_to_all(factors.reshape(pair_size, chunk, aux_count), 'pairs', 0, 0)  37.4 us
    reduce_scatter x1, waiting for transfers between devices, local(): summed = lax.psum_scatter(summed, 'vloop', scatter_dimension=1, tiled=True)  21.6 us
  transfers between devices with their start and end apart: 6, of which 4 were waited for; matrix products, arithmetic and copies ran while one was open for 0% of the time, Pallas kernels for 11%

profile of v1, /device:TPU:0, one launch (start us, length us, event | category | flops | bytes accessed | tf_op | source)
XLA Modules:
  0.0 543.0 jit_solution(14874495998388935653)
XLA Ops:
  6.5 0.0 all-gather.2.cloned.1.call-start
  6.5 37.4 %all_to_all.10 = f32[8,64,1280]{2,1,0:T(8,128)S(1)} all-to-all(f32[8,64,1280]{2,1,0:T(8,128)} %param.5), channel_id=1, replica_groups=mesh['vloop'=4,'pairs'=8] {'pairs'}, dimensions={0} | all-to-all | bytes 5242880 | tf_op jit(solution)/shard_map/all_to_all | solution.py:126
  43.9 63.6 %all_to_all.11 = f32[4,2,64,1280]{3,2,1,0:T(8,128)} all-to-all(f32[4,2,64,1280]{3,2,1,0:T(8,128)S(1)} %bitcast.26), channel_id=1, replica_groups=mesh['vloop'=4,'pairs'=8] {'vloop'}, dimensions={0} | all-to-all | bytes 5242880 | tf_op jit(solution)/shard_map/all_to_all | solution.py:127
  107.5 0.0 copy-start
  107.5 0.0 all-gather.2.cloned.1.call-update
  107.6 0.0 reduce-scatter.3.cloned.1.call-start
  107.6 1.7 copy-done
  109.3 1.4 collective-permute-start.1
  110.7 0.3 collective-permute-start.2
  111.0 0.5 collective-permute-start
  111.4 57.2 %collective-permute-done.1 = f32[8,64,1280]{2,1,0:T(8,128)} collective-permute-done((f32[8,64,1280]{2,1,0:T(8,128)S(1)}, f32[8,64,1280]{2,1,0:T(8,128)}, u32[]{:S(2)}, u32[]{:S(2)}) %collective-permute-start.1) | collective-permute-done | bytes 2621472 | tf_op jit(solution)/shard_map/ppermute | solution.py:148
  168.7 165.9 %collective-permute-done.2 = f32[8,64,1280]{2,1,0:T(8,128)} collective-permute-done((f32[8,64,1280]{2,1,0:T(8,128)S(1)}, f32[8,64,1280]{2,1,0:T(8,128)}, u32[]{:S(2)}, u32[]{:S(2)}) %collective-permute-start.2) | collective-permute-done | bytes 2621472 | tf_op jit(solution)/shard_map/ppermute | solution.py:148
  334.6 0.0 all-gather.2.cloned.1.call-done
  334.6 59.3 %shard_map.56 = f32[256,256]{1,0:T(8,128)} custom-call(f32[32,128,1280]{2,1,0:T(8,128)} %bitcast.38, f32[128,64,128]{2,1,0:T(8,128)} %amp_ref.3, f32[512,1280]{1,0:T(8,128)} %bitcast.8.refs_0_, f32[512,1280]{1,0:T(8,128)} %bitcast.9.refs_1_), custom_call_target="tpu_custom_call" | custom-call | flops 38654705664 | bytes 26214400 | tf_op jit(solution)/shard_map/pallas_call | solution.py:86
  393.9 1.1 reshape.48
  395.1 0.0 collective-permute-done
  395.1 59.3 %shard_map.55 = f32[256,256]{1,0:T(8,128)} custom-call(f32[32,128,1280]{2,1,0:T(8,128)} %bitcast.39, f32[128,64,128]{2,1,0:T(8,128)} %amp_ref.3, f32[512,1280]{1,0:T(8,128)} %bitcast.31, f32[512,1280]{1,0:T(8,128)} %bitcast.4.refs_1_), custom_call_target="tpu_custom_call" | custom-call | flops 38654705664 | bytes 26214400 | tf_op jit(solution)/shard_map/pallas_call | solution.py:86
  454.4 1.1 reshape.45
  455.7 0.1 pad_maximum_fusion.11
  455.7 1.8 copy.35
  457.6 2.8 copy.34
  460.4 2.8 copy.33
  463.2 2.8 copy.32
  466.0 5.9 %pad_maximum_fusion = f32[128,32,4,8]{1,3,2,0:T(8,128)} fusion(f32[128,8,4,8]{1,3,2,0:T(8,128)S(1)} %bitcast.27, f32[128,8,4,8]{1,3,2,0:T(8,128)} %bitcast.28, f32[128,8,4,8]{1,3,2,0:T(8,128)} %bitcast.29, f32[128,8,4,8]{1,3,2,0:T(8,128)} %bitcast.30), kind=kLoop, calls=%fused_computation | loop fusion | flops 393216 | bytes 1048576 | tf_op jit(solution)/shard_map/concatenate | solution.py:168
  471.9 0.0 copy-start.1
  471.9 0.0 copy-start.2
  471.9 0.0 copy-start.3
  471.9 0.0 reduce-scatter.3.cloned.1.call-update
  471.9 0.0 reduce-scatter.5.cloned.1.call-start
  472.0 0.5 copy-done.1
  472.5 0.1 fusion.2
  472.6 38.1 %reduce-scatter.3.cloned.1.call-done = f32[16,32,4,8]{1,3,2,0:T(8,128)} async-done(((f32[128,32,4,8]{1,3,2,0:T(8,128)}), f32[16,32,4,8]{1,3,2,0:T(8,128)}) %reduce-scatter.3.cloned.1.call-update) | async-done | bytes 65552 | tf_op jit(solution)/shard_map/reduce_scatter | solution.py:169
  510.7 2.2 copy.36
  512.9 0.0 reduce-scatter.5.cloned.1.call-update
  512.9 0.1 broadcast_add_fusion
  513.0 0.0 copy-done.2
  513.0 0.0 copy-done.3
  513.0 0.2 select_reduce_fusion
  513.2 21.6 %reduce-scatter.5.cloned.1.call-done = f32[16,8,4,8]{0,3,2,1:T(8,128)} async-done(((f32[16,32,4,8]{0,3,2,1:T(8,128)}), f32[16,8,4,8]{0,3,2,1:T(8,128)}) %reduce-scatter.5.cloned.1.call-update) | async-done | bytes 16400 | tf_op jit(solution)/shard_map/reduce_scatter | solution.py:170
  534.8 1.7 subtract_divide_fusion
  (9 shorter events, 0.2 us)
Async XLA Ops:
  6.5 328.1 %all-gather.2.cloned.1.call-start = ((), (), s32[]{:S(2)}) async-start(), calls=%async_computation.4 | async-start | bytes 23592960 | tf_op jit(solution)/shard_map/all_gather | solution.py:130
  107.5 1.7 copy-start
  107.6 403.2 %reduce-scatter.3.cloned.1.call-start = ((), (), s32[]{:S(2)}) async-start(), calls=%async_computation.5 | async-start | bytes 2359296 | tf_op jit(solution)/shard_map/reduce_scatter | solution.py:169
  109.3 59.4 %collective-permute-start.1 = (f32[8,64,1280]{2,1,0:T(8,128)S(1)}, f32[8,64,1280]{2,1,0:T(8,128)}, u32[]{:S(2)}, u32[]{:S(2)}) collective-permute-start(f32[8,64,1280]{2,1,0:T(8,128)S(1)} %copy-done), channel_id=1, source_target_pairs={{0,24},{8,0},{16,8},{24,16},{1,25},{9,1},{17,9},{25,17},{2,26},{10... | collective-permute-start | bytes 7864328 | tf_op jit(solution)/shard_map/ppermute | solution.py:148
  110.7 223.9 %collective-permute-start.2 = (f32[8,64,1280]{2,1,0:T(8,128)S(1)}, f32[8,64,1280]{2,1,0:T(8,128)}, u32[]{:S(2)}, u32[]{:S(2)}) collective-permute-start(f32[8,64,1280]{2,1,0:T(8,128)S(1)} %copy-done), channel_id=1, source_target_pairs={{0,16},{8,24},{16,0},{24,8},{1,17},{9,25},{17,1},{25,9},{2,18},{10... | collective-permute-start | bytes 7864328 | tf_op jit(solution)/shard_map/ppermute | solution.py:148
  111.0 284.1 %collective-permute-start = (f32[8,64,1280]{2,1,0:T(8,128)S(1)}, f32[8,64,1280]{2,1,0:T(8,128)}, u32[]{:S(2)}, u32[]{:S(2)}) collective-permute-start(f32[8,64,1280]{2,1,0:T(8,128)S(1)} %copy-done), channel_id=1, source_target_pairs={{0,8},{8,16},{16,24},{24,0},{1,9},{9,17},{17,25},{25,1},{2,10},{10... | collective-permute-start | bytes 7864328 | tf_op jit(solution)/shard_map/ppermute | solution.py:148
  471.9 0.7 copy-start.1
  471.9 41.1 %copy-start.2 = (s32[16,2]{0,1:T(2,128)S(1)}, s32[16,2]{0,1:T(2,128)}, u32[]{:S(2)}) copy-start(s32[16,2]{0,1:T(2,128)} %param.9) | copy-start | bytes 388
  471.9 41.1 %copy-start.3 = (f32[96]{0:T(128)S(1)}, f32[96]{0:T(128)}, u32[]{:S(2)}) copy-start(f32[96]{0:T(128)} %param.7) | copy-start | bytes 1156
  471.9 62.9 %reduce-scatter.5.cloned.1.call-start = ((), (), s32[]{:S(2)}) async-start(), calls=%async_computation.6 | async-start | bytes 655360 | tf_op jit(solution)/shard_map/reduce_scatter | solution.py:170
Sparse Core Ops, SparseCore 0:
  107.7 105.7 all-gather.1
  472.0 38.6 reduce-scatter.2
  513.1 21.6 reduce-scatter.4

commit v2 on v1

--- a/solution.py
+++ b/solution.py
@@ -142,17 +142,19 @@
     row_side = row_side.transpose(0, 1, 4, 3, 2, 5, 6)
     row_side = row_side.reshape(loop_size * rows_dev, block_cols, aux_count)
 
-    def shifted(by):
-        if by == 0:
-            return factors
-        return lax.ppermute(factors, "vloop", [(i, (i + by) % loop_size) for i in range(loop_size)])
+    def shifted(block, by):
+        return lax.ppermute(block, "vloop", [(i, (i + by) % loop_size) for i in range(loop_size)])
 
     order = [0, 1, loop_size - 1] + list(range(2, loop_size - 1))
+    blocks_of = {0: factors, 1: shifted(factors, 1), loop_size - 1: shifted(factors, -1)}
+    for by in range(2, loop_size - 1):
+        blocks_of[by] = shifted(blocks_of[by - 1], 1)
     half = loop_size // 2
     found = {}
     for start in (0, half):
         shifts = order[start : start + half]
-        part = ladder_part(row_side, amplitudes, [shifted(by) for by in shifts])
+        part = ladder_part(row_side, amplitudes, [blocks_of[by] for by in shifts])
+        part, amplitudes = lax.optimization_barrier((part, amplitudes))
         for i, by in enumerate(shifts):
             found[by] = part[i]
     stacked = jnp.stack([found[by] for by in range(loop_size)])
@@ -164,10 +166,12 @@
     for z in range(loop_size):
         mine = jnp.stack([blocks[(z - s) % loop_size] for s in range(STEPS)])
         mine = mine[:, :, z * rows_dev : (z + 1) * rows_dev]
-        rows.append(mine.transpose(3, 2, 0, 1))
-    ladder = jnp.concatenate(rows, axis=1)
-    summed = lax.psum_scatter(ladder, "pairs", scatter_dimension=0, tiled=True)
-    summed = lax.psum_scatter(summed, "vloop", scatter_dimension=1, tiled=True)
+        rows.append(mine)
+    ladder = lax.all_to_all(jnp.stack(rows), "vloop", 0, 0)
+    summed = jnp.sum(ladder, axis=0).reshape(-1, rows_dev, pair_count)
+    summed = summed.transpose(2, 1, 0).reshape(pair_size, pair_count // pair_size, -1)
+    summed = jnp.sum(lax.all_to_all(summed, "pairs", 0, 0), axis=0)
+    summed = summed.reshape(-1, rows_dev, STEPS, rows_dev)
 
     one_hot = (
         pair_list[:, :, None] == jnp.arange(occ_energy.shape[0], dtype=jnp.int32)[None, None, :]

time: 543 us -> 377 us (0.69)
  waiting for transfers between devices: 283 us -> 125 us
  local copies, waits for them, and re-layouts: 17 us -> 5.28 us
  starting transfers between devices: 2.25 us -> 10.7 us
  other arithmetic: 7.9 us -> 2.01 us
    ppermute x3, waiting for transfers between devices: 223 us -> 65 us  [shifted(): lax.ppermute(block, 'vloop', [(i, (i + by) % loop_size) for i in range(lo...]
    reduce_scatter x2 -> x0, waiting for transfers between devices: 59.7 us -> none  [the longest x1 38.1 us: local(): summed = lax.psum_scatter(ladder, 'pairs', scatter_dimension=0, tiled=True)]
    all_gather x1, waiting for transfers between devices: 0.01 us -> 42.4 us  [local(): lax.all_gather(spread.reshape(loop_size, 1, per_block * chunk, aux_count)...]
    all_to_all x0 -> x2, waiting for transfers between devices: none -> 17.8 us  [the longest x1 12.6 us: local(): ladder = lax.all_to_all(jnp.stack(rows), 'vloop', 0, 0)]
    slice x4 -> x0, local copies, waits for them, and re-layouts: 10.3 us -> none  [local(): mine = mine[:, :, z * rows_dev:(z + 1) * rows_dev]]
    all_to_all x0 -> x2, starting transfers between devices: none -> 6.84 us  [the longest x1 3.47 us: local(): ladder = lax.all_to_all(jnp.stack(rows), 'vloop', 0, 0)]
    concatenate x1 -> x0, other arithmetic: 5.88 us -> none  [local(): ladder = jnp.concatenate(rows, axis=1)]
  transfers between devices with their start and end apart: 6 -> 6, of which waited for: 4 -> 5; matrix products, arithmetic and copies ran while one was open for 0% -> 0% of each run, Pallas kernels for 11% -> 16%
where the time goes in v2:
time: 377 us; the launch traced here: 376 us
  waiting for transfers between devices  125 us (33%)
  Pallas kernels  119 us (32%)
  blocking collectives  101 us (27%)
  between operations  13.6 us (4%)
  starting transfers between devices  10.7 us (3%)
  local copies, waits for them, and re-layouts  5.28 us (1%)
    pallas_call x2, Pallas kernels, ladder_part(): pl.pallas_call(functools.partial(ladder_kernel, count), grid=(all_c // ti...  119 us
    ppermute x3, waiting for transfers between devices, shifted(): lax.ppermute(block, 'vloop', [(i, (i + by) % loop_size) for i in range(lo...  65 us
    all_to_all x1, blocking collectives, local(): lax.all_to_all(spread.reshape(loop_size, per_block, chunk, aux_count), 'v...  63.6 us
    all_gather x1, waiting for transfers between devices, local(): lax.all_gather(spread.reshape(loop_size, 1, per_block * chunk, aux_count)...  42.4 us
    all_to_all x1, blocking collectives, local(): lax.all_to_all(factors.reshape(pair_size, chunk, aux_count), 'pairs', 0, 0)  37.4 us
    all_to_all x1, waiting for transfers between devices, local(): ladder = lax.all_to_all(jnp.stack(rows), 'vloop', 0, 0)  12.6 us
  transfers between devices with their start and end apart: 6, of which 5 were waited for; matrix products, arithmetic and copies ran while one was open for 0% of the time, Pallas kernels for 16%

profile of v2, /device:TPU:0, one launch (start us, length us, event | category | flops | bytes accessed | tf_op | source)
XLA Modules:
  0.0 376.4 jit_solution(12072430561228373212)
XLA Ops:
  6.5 0.0 all-gather.2.cloned.1.call-start
  6.5 37.4 %all_to_all.20 = f32[8,64,1280]{2,1,0:T(8,128)S(1)} all-to-all(f32[8,64,1280]{2,1,0:T(8,128)} %param.5), channel_id=1, replica_groups=mesh['vloop'=4,'pairs'=8] {'pairs'}, dimensions={0} | all-to-all | bytes 5242880 | tf_op jit(solution)/shard_map/all_to_all | solution.py:126
  43.9 63.6 %all_to_all.21 = f32[4,2,64,1280]{3,2,1,0:T(8,128)} all-to-all(f32[4,2,64,1280]{3,2,1,0:T(8,128)S(1)} %bitcast.34), channel_id=1, replica_groups=mesh['vloop'=4,'pairs'=8] {'vloop'}, dimensions={0} | all-to-all | bytes 5242880 | tf_op jit(solution)/shard_map/all_to_all | solution.py:127
  107.5 0.0 copy-start
  107.5 0.0 all-gather.2.cloned.1.call-update
  107.6 1.7 copy-done
  109.3 0.2 collective-permute-start
  109.5 3.6 collective-permute-start.1
  113.1 57.9 %collective-permute-done = f32[8,64,1280]{2,1,0:T(8,128)} collective-permute-done((f32[8,64,1280]{2,1,0:T(8,128)S(1)}, f32[8,64,1280]{2,1,0:T(8,128)}, u32[]{:S(2)}, u32[]{:S(2)}) %collective-permute-start) | collective-permute-done | bytes 2621472 | tf_op jit(solution)/shard_map/ppermute | solution.py:146
  171.0 0.0 collective-permute-start.2
  171.0 42.4 %all-gather.2.cloned.1.call-done = f32[4,8,128,1280]{3,2,1,0:T(8,128)} async-done(((f32[4,1,128,1280]{3,2,1,0:T(8,128)}), f32[4,8,128,1280]{3,2,1,0:T(8,128)}) %all-gather.2.cloned.1.call-update) | async-done | bytes 20971536 | tf_op jit(solution)/shard_map/all_gather | solution.py:130
  213.4 59.3 %shard_map.55 = f32[256,256]{1,0:T(8,128)} custom-call(f32[32,128,1280]{2,1,0:T(8,128)} %bitcast.40, f32[128,64,128]{2,1,0:T(8,128)} %amp_ref.2, f32[512,1280]{1,0:T(8,128)} %bitcast.35, f32[512,1280]{1,0:T(8,128)} %bitcast.4.refs_1_), custom_call_target="tpu_custom_call" | custom-call | flops 38654705664 | bytes 26214400 | tf_op jit(solution)/shard_map/pallas_call | solution.py:86
  272.7 1.1 reshape.54
  273.8 0.0 collective-permute-done.1
  273.9 7.1 %collective-permute-done.2 = f32[8,64,1280]{2,1,0:T(8,128)} collective-permute-done((f32[8,64,1280]{2,1,0:T(8,128)}, f32[8,64,1280]{2,1,0:T(8,128)}, u32[]{:S(2)}, u32[]{:S(2)}) %collective-permute-start.2) | collective-permute-done | bytes 2621472 | tf_op jit(solution)/shard_map/ppermute | solution.py:146
  281.0 59.3 %shard_map.56 = f32[256,256]{1,0:T(8,128)} custom-call(f32[32,128,1280]{2,1,0:T(8,128)} %bitcast.41, f32[128,64,128]{2,1,0:T(8,128)} %amp_ref.2, f32[512,1280]{1,0:T(8,128)} %bitcast.7.refs_0_, f32[512,1280]{1,0:T(8,128)} %bitcast.8.refs_1_), custom_call_target="tpu_custom_call" | custom-call | flops 38654705664 | bytes 26214400 | tf_op jit(solution)/shard_map/pallas_call | solution.py:86
  340.3 1.1 reshape.58
  341.4 0.0 copy-start.1
  341.5 0.0 copy-start.2
  341.5 0.0 copy-start.3
  341.5 0.1 fusion.3
  341.6 0.9 pad_maximum_fusion.1
  342.4 3.5 all-to-all-start.2
  346.0 0.0 copy-done.1
  346.0 0.1 fusion.5
  346.1 12.6 %all-to-all-done.2 = f32[4,4,8,8,128]{4,3,2,1,0:T(8,128)S(1)} async-done(((f32[4,4,8,8,128]{4,3,2,1,0:T(8,128)}), f32[4,4,8,8,128]{4,3,2,1,0:T(8,128)S(1)}, u32[]{:S(2)}, u32[]{:S(2)}) %all-to-all-start.2) | async-done | bytes 524320 | tf_op jit(solution)/shard_map/all_to_all | solution.py:170
  358.7 0.2 copy.26
  359.0 0.8 reshape.61
  359.8 3.4 all-to-all-start.3
  363.2 0.1 broadcast_add_fusion
  363.3 0.0 copy-done.2
  363.3 0.0 copy-done.3
  363.3 0.2 select_reduce_fusion
  363.5 5.2 %all-to-all-done.3 = f32[8,16,256]{2,1,0:T(8,128)S(1)} async-done(((f32[8,16,256]{2,1,0:T(8,128)}), f32[8,16,256]{2,1,0:T(8,128)S(1)}, u32[]{:S(2)}, u32[]{:S(2)}) %all-to-all-start.3) | async-done | bytes 131104 | tf_op jit(solution)/shard_map/all_to_all | solution.py:173
  368.7 0.1 copy.27
  368.8 0.8 subtract_divide_fusion
  (8 shorter events, 0.2 us)
Async XLA Ops:
  6.5 206.9 %all-gather.2.cloned.1.call-start = ((), (), s32[]{:S(2)}) async-start(), calls=%async_computation.4 | async-start | bytes 23592960 | tf_op jit(solution)/shard_map/all_gather | solution.py:130
  107.5 1.7 copy-start
  109.3 61.7 %collective-permute-start = (f32[8,64,1280]{2,1,0:T(8,128)S(1)}, f32[8,64,1280]{2,1,0:T(8,128)}, u32[]{:S(2)}, u32[]{:S(2)}) collective-permute-start(f32[8,64,1280]{2,1,0:T(8,128)S(1)} %copy-done), channel_id=1, source_target_pairs={{0,8},{8,16},{16,24},{24,0},{1,9},{9,17},{17,25},{25,1},{2,10},{10... | collective-permute-start | bytes 7864328 | tf_op jit(solution)/shard_map/ppermute | solution.py:146
  109.5 164.4 %collective-permute-start.1 = (f32[8,64,1280]{2,1,0:T(8,128)S(1)}, f32[8,64,1280]{2,1,0:T(8,128)}, u32[]{:S(2)}, u32[]{:S(2)}) collective-permute-start(f32[8,64,1280]{2,1,0:T(8,128)S(1)} %copy-done), channel_id=1, source_target_pairs={{0,24},{8,0},{16,8},{24,16},{1,25},{9,1},{17,9},{25,17},{2,26},{10... | collective-permute-start | bytes 7864328 | tf_op jit(solution)/shard_map/ppermute | solution.py:146
  171.0 110.0 %collective-permute-start.2 = (f32[8,64,1280]{2,1,0:T(8,128)}, f32[8,64,1280]{2,1,0:T(8,128)}, u32[]{:S(2)}, u32[]{:S(2)}) collective-permute-start(f32[8,64,1280]{2,1,0:T(8,128)} %collective-permute-done), channel_id=1, source_target_pairs={{0,8},{8,16},{16,24},{24,0},{1,9},{9,17},{17,25},{25,1},{2,10},{10... | collective-permute-start | bytes 7864328 | tf_op jit(solution)/shard_map/ppermute | solution.py:146
  341.4 4.6 %copy-start.1 = (f32[32]{0:T(128)S(1)}, f32[32]{0:T(128)}, u32[]{:S(2)}) copy-start(f32[32]{0:T(128)} %param.8) | copy-start | bytes 388
  341.5 21.8 %copy-start.2 = (s32[16,2]{0,1:T(2,128)S(1)}, s32[16,2]{0,1:T(2,128)}, u32[]{:S(2)}) copy-start(s32[16,2]{0,1:T(2,128)} %param.9) | copy-start | bytes 388
  341.5 21.8 %copy-start.3 = (f32[96]{0:T(128)S(1)}, f32[96]{0:T(128)}, u32[]{:S(2)}) copy-start(f32[96]{0:T(128)} %param.7) | copy-start | bytes 1156
  342.4 16.3 %all-to-all-start.2 = ((f32[4,4,8,8,128]{4,3,2,1,0:T(8,128)}), f32[4,4,8,8,128]{4,3,2,1,0:T(8,128)S(1)}, u32[]{:S(2)}, u32[]{:S(2)}) async-start(f32[4,4,8,8,128]{4,3,2,1,0:T(8,128)} %pad_maximum_fusion.1), calls=%async_computation.2 | async-start | bytes 1048576 | tf_op jit(solution)/shard_map/all_to_all | solution.py:170
  359.8 8.8 %all-to-all-start.3 = ((f32[8,16,256]{2,1,0:T(8,128)}), f32[8,16,256]{2,1,0:T(8,128)S(1)}, u32[]{:S(2)}, u32[]{:S(2)}) async-start(f32[8,16,256]{2,1,0:T(8,128)} %reshape.61), calls=%async_computation.3 | async-start | bytes 262144 | tf_op jit(solution)/shard_map/all_to_all | solution.py:173
Sparse Core Ops, SparseCore 0:
  107.7 105.7 all-gather.1
